TPU v7x, 512 devices: a whole 4x4x16 slice. The times are simulated.
512 devices in a mesh: chan: 128 (over z, x, core), blk: 4 (over y).
Axes of the slice: x: 4, y: 4, z: 16, core: 2. Of those that a mesh axis runs over, the one named last changes fastest.
Arguments:
- omega: float32 [128, 576, 576], P('chan', 'blk'), may hold values from -0.25 to 0.25
- hamiltonian: float32 [128, 576, 576], P('chan', 'blk'), may hold values from -6 to 6
- pair_occ: float32 [128, 576], P('chan'), may hold values from -1 to 1
- cross_occ: float32 [128, 576], P('chan'), may hold values from -1 to 1
- block_size: int32 [128], P('chan'), may hold values from 288 to 576
- jlabel: int32 [128], replicated, may hold values from 0 to 127
- family: int32 [128], replicated, may hold values from 0 to 3
- sixj: float32 [128, 128], replicated, may hold values from -1 to 1
- column_map: int32 [576], replicated, may hold values from 0 to 575, each once
Outputs:
- evolved: float32 [128, 576, 576], P('chan', 'blk')
Inputs may be any that keep to these rules, and one draw needn't show every extreme that they name: `column_map`: a permutation of 0 to 575.
All inputs are finite; a program needn't handle non-finite values.
Results may differ from a plain program's by a relative error of at most 0.0032.
Values may be sent and summed in bfloat16 or wider, within the bound.
A program may use at most 64 MiB of HBM per device.

v0:
```python
import jax
import jax.numpy as jnp
from jax import lax
from jax.sharding import PartitionSpec as P

exact_mode = lax.Precision.HIGHEST


def in_order(parts, dim):
    parts = jnp.moveaxis(parts, 0, dim)
    lengths = parts.shape
    return parts.reshape(*lengths[:dim], lengths[dim] * lengths[dim + 1], *lengths[dim + 2 :])


def copy_for_each(shard, axis):
    copies = jnp.broadcast_to(shard, (lax.axis_size(axis), *shard.shape))
    return lax.all_to_all(copies, axis, split_axis=0, concat_axis=0, tiled=True)


def gather_directly(shard, axis, dim):
    return in_order(copy_for_each(shard, axis), dim)


def mixing_matrix(jlabel, family, sixj):
    levels = sixj.shape[0]
    one_hot = (jlabel[:, None] == jnp.arange(levels, dtype=jnp.int32)[None, :]).astype(jnp.float32)
    picked = jnp.dot(one_hot, sixj, precision=exact_mode, preferred_element_type=jnp.float32)
    picked = jnp.dot(picked, one_hot.T, precision=exact_mode, preferred_element_type=jnp.float32)
    kindred = (family[:, None] == family[None, :]).astype(jnp.float32)
    return picked * kindred


def commutator(left_rows, left_full, right_rows, weights):
    scaled_left = (left_rows * weights[:, None, :]).astype(jnp.bfloat16)
    scaled_right = (right_rows * weights[:, None, :]).astype(jnp.bfloat16)
    initial = -jnp.einsum(
        "crk,ckq->crq", scaled_right, left_full, preferred_element_type=jnp.float32
    )
    return initial + jnp.einsum(
        "crk,ckq->crq",
        scaled_left,
        lax.all_gather(right_rows.astype(jnp.bfloat16), "blk", axis=1, tiled=True),
        preferred_element_type=jnp.float32,
    )


def through_mixing(stacked, apply_fn):
    chan_size = lax.axis_size("chan")
    members, channels_here, rows_here, block_width = stacked.shape
    shaped = stacked.reshape(
        members, channels_here, chan_size, rows_here * block_width // chan_size
    )
    returned = lax.all_to_all(
        apply_fn(lax.all_to_all(shaped, "chan", split_axis=2, concat_axis=1, tiled=True)),
        "chan",
        split_axis=1,
        concat_axis=2,
        tiled=True,
    )
    return returned.reshape(returned.shape[0], channels_here, rows_here, block_width)


def on_device(
    omega, hamiltonian, pair_occ, cross_occ, block_size, jlabel, family, sixj, column_map
):
    channels_here, rows_here, block_width = omega.shape
    mixing = mixing_matrix(jlabel, family, sixj)
    row_index = lax.axis_index("blk") * rows_here + jnp.arange(rows_here, dtype=jnp.int32)
    col_index = jnp.arange(block_width, dtype=jnp.int32)
    inside_block = (row_index[None, :, None] < block_size[:, None, None]) & (
        col_index[None, None, :] < block_size[:, None, None]
    )
    window_mask = inside_block.astype(jnp.float32)
    generator = omega * window_mask
    start_ham = hamiltonian * window_mask
    inverse_map = jnp.argsort(column_map)

    def forward_mix(received):
        return jnp.einsum(
            "kc,scil->skil",
            mixing,
            received,
            precision=exact_mode,
            preferred_element_type=jnp.float32,
        )

    def reverse_mix(received):
        return jnp.einsum(
            "ck,scil->skil",
            mixing,
            received,
            precision=exact_mode,
            preferred_element_type=jnp.float32,
        )

    crossed = through_mixing(
        jnp.stack([generator[:, :, column_map], start_ham[:, :, column_map]]), forward_mix
    )
    gen_cross = crossed[0]
    ham_cross = crossed[1]
    gen_full = lax.all_gather(generator.astype(jnp.bfloat16), "blk", axis=1, tiled=True)
    first_pp = commutator(generator, gen_full, start_ham, pair_occ)
    cross_full = gather_directly(gen_cross.astype(jnp.bfloat16), "blk", 1)
    first_cc = commutator(gen_cross, cross_full, ham_cross, cross_occ)

    def both_mix(received):
        restored = jnp.einsum(
            "ck,cil->kil",
            mixing,
            received[1],
            precision=exact_mode,
            preferred_element_type=jnp.float32,
        )
        combined = jnp.einsum(
            "kc,cil->kil",
            mixing,
            received[0] + restored,
            precision=exact_mode,
            preferred_element_type=jnp.float32,
        )
        return jnp.stack([restored, combined])

    outcome = through_mixing(jnp.stack([first_pp[:, :, column_map], first_cc]), both_mix)
    eta = first_pp + outcome[0][:, :, inverse_map]
    eta_cross = outcome[1]
    second_pp = commutator(generator, gen_full, eta, pair_occ)
    second_cc = commutator(gen_cross, cross_full, eta_cross, cross_occ)
    second_back = through_mixing(second_cc[None], reverse_mix)[0]
    second = second_pp + second_back[:, :, inverse_map]
    return (start_ham + eta + 0.5 * second) * window_mask


def solution(mesh):
    in_specs = (
        P("chan", "blk", None),
        P("chan", "blk", None),
        P("chan", None),
        P("chan", None),
        P("chan"),
        P(),
        P(),
        P(),
        P(),
    )
    out_specs = P("chan", "blk", None)
    return jax.shard_map(
        on_device, mesh=mesh, in_specs=in_specs, out_specs=out_specs, check_vma=False
    )
```

profile of v0, /device:TPU:1, one launch (start us, length us, event | category | flops | bytes accessed | tf_op | source)
XLA Modules:
  0.0 369.2 jit_solution(17199406350710039180)
XLA Ops:
  2.2 2.2 gather_fusion.1
  5.2 2.2 gather_fusion.2
  8.1 1.5 copy.68
  9.6 20.5 %all-to-all-start = ((f32[2,1,128,648]{3,0,1,2:T(2,128)}), f32[2,1,128,648]{3,0,1,2:T(2,128)S(1)}, u32[]{:S(2)}, u32[]{:S(2)}) async-start(f32[2,1,128,648]{3,0,1,2:T(2,128)} %copy.68), calls=%async_computation | async-start | bytes 1572864 | tf_op jit(solution)/shard_map/all_to_all | solution.py:54
  30.7 40.9 %all-to-all-done = f32[2,1,128,648]{3,0,1,2:T(2,128)S(1)} async-done(((f32[2,1,128,648]{3,0,1,2:T(2,128)}), f32[2,1,128,648]{3,0,1,2:T(2,128)S(1)}, u32[]{:S(2)}, u32[]{:S(2)}) %all-to-all-start) | async-done | bytes 663584 | tf_op jit(solution)/shard_map/all_to_all | solution.py:54
  74.1 10.0 %all-to-all-start.1 = ((f32[2,128,1,648]{3,0,2,1:T(2,128)}), f32[2,128,1,648]{3,0,2,1:T(2,128)}, u32[]{:S(2)}, u32[]{:S(2)}) async-start(f32[2,128,1,648]{3,0,2,1:T(2,128)} %copy.70), calls=%async_computation.1 | async-start | bytes 1572864 | tf_op jit(solution)/shard_map/all_to_all | solution.py:53
  86.1 12.9 %all_gather.15 = bf16[1,576,576]{2,1,0:T(8,128)(2,1)S(1)} all-gather(bf16[1,144,576]{2,1,0:T(8,128)(2,1)S(1)} %get-tuple-element.17), channel_id=1, replica_groups=mesh['chan'=128,'blk'=4] {'blk'}, dimensions={1}, use_global_device_ids=true | all-gather | bytes 829440 | tf_op jit(solution)/shard_map/all_gather | solution.py:101
  99.0 11.7 %all_gather.16 = bf16[1,576,576]{2,1,0:T(8,128)(2,1)S(1)} all-gather(bf16[1,144,576]{2,1,0:T(8,128)(2,1)S(1)} %get-tuple-element.18), channel_id=1, replica_groups=mesh['chan'=128,'blk'=4] {'blk'}, dimensions={1}, use_global_device_ids=true | all-gather | bytes 829440 | tf_op jit(solution)/shard_map/all_gather | solution.py:42
  111.8 2.2 gather_fusion
  115.3 10.0 %all-to-all-done.1 = f32[2,128,1,648]{3,0,2,1:T(2,128)} async-done(((f32[2,128,1,648]{3,0,2,1:T(2,128)}), f32[2,128,1,648]{3,0,2,1:T(2,128)}, u32[]{:S(2)}, u32[]{:S(2)}) %all-to-all-start.1) | async-done | bytes 663584 | tf_op jit(solution)/shard_map/all_to_all | solution.py:53
  125.3 2.0 fusion.44
  133.1 4.3 %all-to-all-start.2 = ((bf16[4,1,144,576]{3,2,1,0:T(8,128)(2,1)}), bf16[4,1,144,576]{3,2,1,0:T(8,128)(2,1)S(1)}, u32[]{:S(2)}, u32[]{:S(2)}) async-start(bf16[4,1,144,576]{3,2,1,0:T(8,128)(2,1)} %broadcast_in_dim.7), calls=%async_computation.2 | async-start | bytes 1474560 | tf_op jit(solution)/shard_map/all_to_all | solution.py:17
  137.4 16.7 %all_gather.17 = bf16[1,576,576]{2,1,0:T(8,128)(2,1)S(1)} all-gather(bf16[1,144,576]{2,1,0:T(8,128)(2,1)S(1)} %copy-done.12), channel_id=1, replica_groups=mesh['chan'=128,'blk'=4] {'blk'}, dimensions={1}, use_global_device_ids=true | all-gather | bytes 829440 | tf_op jit(solution)/shard_map/all_gather | solution.py:42
  158.4 55.3 %all_to_all.28 = f32[2,1,128,648]{3,1,0,2:T(1,128)S(1)} all-to-all(f32[2,1,128,648]{3,1,0,2:T(1,128)S(1)} %copy.73), channel_id=1, replica_groups=mesh['chan'=128,'blk'=4] {'chan'}, dimensions={2} | all-to-all | bytes 1327104 | tf_op jit(solution)/shard_map/all_to_all | solution.py:54
  218.5 2.3 copy.76
  220.8 50.7 %all_to_all.29 = f32[2,128,1,648]{3,2,0,1:T(1,128)S(1)} all-to-all(f32[2,128,1,648]{3,2,0,1:T(1,128)S(1)} %copy.76), channel_id=1, replica_groups=mesh['chan'=128,'blk'=4] {'chan'}, dimensions={1} | all-to-all | bytes 1327104 | tf_op jit(solution)/shard_map/all_to_all | solution.py:53
  274.5 11.1 %all_gather.19 = bf16[1,576,576]{2,1,0:T(8,128)(2,1)S(1)} all-gather(bf16[1,144,576]{2,1,0:T(8,128)(2,1)S(1)} %convert_element_type.111), channel_id=1, replica_groups=mesh['chan'=128,'blk'=4] {'blk'}, dimensions={1}, use_global_device_ids=true | all-gather | bytes 829440 | tf_op jit(solution)/shard_map/all_gather | solution.py:42
  287.6 37.8 %all_to_all.30 = f32[1,1,128,648]{3,1,0,2:T(1,128)S(1)} all-to-all(f32[1,1,128,648]{3,1,0,2:T(1,128)S(1)} %reshape_broadcast_in_dim.4), channel_id=1, replica_groups=mesh['chan'=128,'blk'=4] {'chan'}, dimensions={2} | all-to-all | bytes 663552 | tf_op jit(solution)/shard_map/all_to_all | solution.py:54
  328.0 8.9 %all-to-all-start.6 = ((f32[1,128,1,648]{3,2,0,1:T(1,128)}), f32[1,128,1,648]{3,2,0,1:T(1,128)S(1)}, u32[]{:S(2)}, u32[]{:S(2)}) async-start(f32[1,128,1,648]{3,2,0,1:T(1,128)} %copy.82), calls=%async_computation.6 | async-start | bytes 786432 | tf_op jit(solution)/shard_map/all_to_all | solution.py:53
  337.6 4.4 %sort.17 = (s32[576]{0:T(1024)}, s32[576]{0:T(1024)S(1)}) sort(s32[576]{0:T(1024)S(1)} %copy-done.18, s32[576]{0:T(1024)S(1)} %iota.20), dimensions={0}, to_apply=%region_0.0 | sort | flops 5760 | bytes 9216 | tf_op jit(solution)/shard_map/jit(argsort)/sort | solution.py:76
  342.6 2.2 gather_fusion.3
  345.0 11.5 %all-gather = bf16[576,576]{1,0:T(8,128)(2,1)S(1)} all-gather(bf16[144,576]{1,0:T(8,128)(2,1)S(1)} %fusion.33), channel_id=2, replica_groups=mesh['chan'=128,'blk'=4] {'blk'}, dimensions={0}, use_global_device_ids=true | all-gather | bytes 829440 | tf_op jit(solution)/shard_map/all_gather | solution.py:42
  357.7 4.7 %all-to-all-done.6 = f32[1,128,1,648]{3,2,0,1:T(1,128)S(1)} async-done(((f32[1,128,1,648]{3,2,0,1:T(1,128)}), f32[1,128,1,648]{3,2,0,1:T(1,128)S(1)}, u32[]{:S(2)}, u32[]{:S(2)}) %all-to-all-start.6) | async-done | bytes 331808 | tf_op jit(solution)/shard_map/all_to_all | solution.py:53
  363.9 2.8 gather_fusion.4
  (117 shorter events, 39.2 us)
Async XLA Ops:
  0.0 30.1 %copy-start = (f32[128,128]{1,0:T(8,128)S(1)}, f32[128,128]{1,0:T(8,128)}, u32[]{:S(2)}) copy-start(f32[128,128]{1,0:T(8,128)} %param.16) | copy-start | bytes 196612
  0.7 110.4 %copy-start.13 = (pred[576]{0:T(1024)(128)(4,1)}, pred[576]{0:T(1024)(128)(4,1)S(1)}, u32[]{:S(2)}) copy-start(pred[576]{0:T(1024)(128)(4,1)S(1)} %iota_compare_fusion.3) | copy-start | bytes 1732
  0.8 110.4 %copy-start.15 = (pred[144]{0:T(512)(128)(4,1)}, pred[144]{0:T(512)(128)(4,1)S(1)}, u32[]{:S(2)}) copy-start(pred[144]{0:T(512)(128)(4,1)S(1)} %add_compare_fusion) | copy-start | bytes 436
  9.6 20.5 %copy-start.21 = (s32[128]{0:T(128)S(1)}, s32[128]{0:T(128)}, u32[]{:S(2)}) copy-start(s32[128]{0:T(128)} %param.14) | copy-start | bytes 1540
  9.6 20.8 %copy-start.22 = (s32[128]{0:T(128)S(1)}, s32[128]{0:T(128)}, u32[]{:S(2)}) copy-start(s32[128]{0:T(128)} %param.15) | copy-start | bytes 1540
  9.6 61.9 %all-to-all-start = ((f32[2,1,128,648]{3,0,1,2:T(2,128)}), f32[2,1,128,648]{3,0,1,2:T(2,128)S(1)}, u32[]{:S(2)}, u32[]{:S(2)}) async-start(f32[2,1,128,648]{3,0,1,2:T(2,128)} %copy.68), calls=%async_computation | async-start | bytes 1572864 | tf_op jit(solution)/shard_map/all_to_all | solution.py:54
  74.1 10.0 %copy-start.19 = (f32[1,576]{1,0:T(1,128)S(1)}, f32[1,576]{1,0:T(1,128)}, u32[]{:S(2)}) copy-start(f32[1,576]{1,0:T(1,128)} %param.11) | copy-start | bytes 6916
  74.1 51.1 %all-to-all-start.1 = ((f32[2,128,1,648]{3,0,2,1:T(2,128)}), f32[2,128,1,648]{3,0,2,1:T(2,128)}, u32[]{:S(2)}, u32[]{:S(2)}) async-start(f32[2,128,1,648]{3,0,2,1:T(2,128)} %copy.70), calls=%async_computation.1 | async-start | bytes 1572864 | tf_op jit(solution)/shard_map/all_to_all | solution.py:53
  84.9 1.0 copy-start.1
  84.9 1.1 copy-start.2
  86.0 43.2 %copy-start.3 = (f32[1,128,1,648]{3,1,2,0:T(8,128)}, f32[1,128,1,648]{3,1,2,0:T(8,128)S(1)}, u32[]{:S(2)}) copy-start(f32[1,128,1,648]{3,1,2,0:T(8,128)S(1)} %mul.105) | copy-start | bytes 995332
  132.1 22.0 %copy-start.5 = (bf16[144,576]{1,0:T(8,128)(2,1)}, bf16[144,576]{1,0:T(8,128)(2,1)S(1)}, u32[]{:S(2)}) copy-start(bf16[144,576]{1,0:T(8,128)(2,1)S(1)} %convert_element_type.102) | copy-start | bytes 497668
  133.1 4.3 %copy-start.12 = (bf16[1,144,576]{2,1,0:T(8,128)(2,1)S(1)}, bf16[1,144,576]{2,1,0:T(8,128)(2,1)}, u32[]{:S(2)}) copy-start(bf16[1,144,576]{2,1,0:T(8,128)(2,1)} %convert_element_type.104) | copy-start | bytes 497668
  133.1 21.4 %all-to-all-start.2 = ((bf16[4,1,144,576]{3,2,1,0:T(8,128)(2,1)}), bf16[4,1,144,576]{3,2,1,0:T(8,128)(2,1)S(1)}, u32[]{:S(2)}, u32[]{:S(2)}) async-start(bf16[4,1,144,576]{3,2,1,0:T(8,128)(2,1)} %broadcast_in_dim.7), calls=%async_computation.2 | async-start | bytes 1474560 | tf_op jit(solution)/shard_map/all_to_all | solution.py:17
  154.1 0.9 copy-start.10
  156.1 1.4 copy-start.7
  215.9 1.0 copy-start.9
  271.5 1.3 copy-start.4
  274.5 11.1 %copy-start.6 = (bf16[144,576]{1,0:T(8,128)(2,1)S(1)}, bf16[144,576]{1,0:T(8,128)(2,1)}, u32[]{:S(2)}) copy-start(bf16[144,576]{1,0:T(8,128)(2,1)} %copy-done.5) | copy-start | bytes 497668
  285.6 0.9 copy-start.11
  328.0 34.4 %all-to-all-start.6 = ((f32[1,128,1,648]{3,2,0,1:T(1,128)}), f32[1,128,1,648]{3,2,0,1:T(1,128)S(1)}, u32[]{:S(2)}, u32[]{:S(2)}) async-start(f32[1,128,1,648]{3,2,0,1:T(1,128)} %copy.82), calls=%async_computation.6 | async-start | bytes 786432 | tf_op jit(solution)/shard_map/all_to_all | solution.py:53
  345.0 11.5 %copy-start.14 = (pred[576]{0:T(1024)(128)(4,1)S(1)}, pred[576]{0:T(1024)(128)(4,1)}, u32[]{:S(2)}) copy-start(pred[576]{0:T(1024)(128)(4,1)} %copy-done.13) | copy-start | bytes 1732
  345.0 11.5 %copy-start.16 = (pred[144]{0:T(512)(128)(4,1)S(1)}, pred[144]{0:T(512)(128)(4,1)}, u32[]{:S(2)}) copy-start(pred[144]{0:T(512)(128)(4,1)} %copy-done.15) | copy-start | bytes 436
  366.7 1.3 copy-start.8
  (3 other events, 2.1 us)
where the time goes:
time: 372 us; the launch traced here: 369 us
  blocking collectives  208 us (56%)
  waiting for transfers between devices  55.5 us (15%)
  local copies, waits for them, and re-layouts  44.6 us (12%)
  starting transfers between devices  43.8 us (12%)
  matrix products  8.38 us (2%)
  other arithmetic  7.91 us (2%)
    all_to_all x2, blocking collectives, through_mixing(): lax.all_to_all(shaped, 'chan', split_axis=2, concat_axis=1, tiled=True)  93.1 us
    all_gather x4, blocking collectives, commutator(): lax.all_gather(right_rows.astype(jnp.bfloat16), 'blk', axis=1, tiled=True)  51 us
    all_to_all x1, blocking collectives, through_mixing(): lax.all_to_all(apply_fn(lax.all_to_all(shaped, 'chan', split_axis=2, conc...  50.7 us
    all_to_all x1, waiting for transfers between devices, through_mixing(): lax.all_to_all(shaped, 'chan', split_axis=2, concat_axis=1, tiled=True)  40.9 us
    all_to_all x1, starting transfers between devices, through_mixing(): lax.all_to_all(shaped, 'chan', split_axis=2, concat_axis=1, tiled=True)  20.5 us
    all_to_all x2, starting transfers between devices, through_mixing(): lax.all_to_all(apply_fn(lax.all_to_all(shaped, 'chan', split_axis=2, conc...  18.9 us
    all_to_all x2, waiting for transfers between devices, through_mixing(): lax.all_to_all(apply_fn(lax.all_to_all(shaped, 'chan', split_axis=2, conc...  14.6 us
    all_gather x1, blocking collectives, on_device(): lax.all_gather(generator.astype(jnp.bfloat16), 'blk', axis=1, tiled=True)  12.9 us
  transfers between devices with their start and end apart: 4, of which 3 were waited for; matrix products, arithmetic and copies ran while one was open for 4% of the time, Pallas kernels for 0%

commit v1 on v0

v1 whole, which is shorter than its diff:
```python
import math

import jax
import jax.numpy as jnp
from jax import lax
from jax.experimental import pallas as pl
from jax.experimental.pallas import tpu as pltpu
from jax.sharding import PartitionSpec as P

F32 = jnp.float32
BF16 = jnp.bfloat16
I32 = jnp.int32
MESH = pl.DeviceIdType.MESH

C = 128
L = 8
Y = 4
ROWS = 144
WIDTH = 576
WIDE = 640
PER = 3
OWNERS = 112
WORDS = OWNERS * PER
TAIL = 288
LAST = 328

G, H, PP, CC, SO = range(5)
GB, HB, EB, RB, SB = range(5)
YG, YH, YGC, YHC, YE, YEC = range(6)

FLOOR = -126.0
OUT_TOP = (0.25, 6.0, 2.0**11, 2.0**26, 2.0**55)
BACK_TOP = (2.0**6, 2.0**11, 2.0**40, 2.0**34, 2.0**63)


def per_octave(top):
    return 32766.0 / (math.log2(top) - FLOOR)


def dot(a, b):
    return jnp.dot(a, b, preferred_element_type=F32)


def halves(value):
    high = value.astype(BF16)
    return high, (value - high.astype(F32)).astype(BF16)


def encode(value, top):
    scale = per_octave(top)
    size = jnp.maximum(jnp.abs(value), 2.0**FLOOR)
    code = jnp.minimum(jnp.round((jnp.log2(size) - FLOOR) * scale), 32767.0)
    return jnp.where(value < 0, -code, code).astype(I32)


def decode(code, top):
    value = code.astype(F32)
    size = jnp.exp2(jnp.abs(value) * (1.0 / per_octave(top)) + FLOOR)
    size = jnp.where(value < 0, -size, size)
    return jnp.where(value == 0, 0.0, size)


def pack(first, second):
    return lax.shift_left(first, 16) | (second & 0xFFFF)


def unpack(word):
    first = lax.shift_right_arithmetic(word, 16)
    return first, lax.shift_right_arithmetic(lax.shift_left(word, 16), 16)


def kernel(
    omega_hbm, ham_hbm, pair_w, cross_w, block, jrow, frow, sixj, cmap,
    out,
    os_ref, or_ref, bs_ref, br_ref,
    full, perm, unperm, mix_hi, mix_lo, rev_hi, rev_lo, sq_hi, sq_lo,
    wide_ref, block_ref, tail_ref, x_hi, x_lo,
    gen_ref, ham_ref, pp_ref, comb_ref, gen_s, ham_s, gc_s, hc_s, eta_ref,
    in_sem, os_sem, or_sem, bs_sem, br_sem, ys_sem, yr_sem,
):
    me = lax.axis_index("chan")
    y = lax.axis_index("blk")
    z = me // L
    lane = lax.rem(me, L)
    place = lax.rem(lane - z - 1 + 3 * L, L)
    owns = place < L - 1
    idle = place == L - 1
    mine = z * (L - 1) + jnp.minimum(place, L - 2)
    idle_n = place // (L - 1)
    y_next = lax.rem(y + 1, Y)
    y_last = lax.rem(y + Y - 1, Y)

    barrier = pltpu.get_barrier_semaphore()

    def greet(step, _):
        to = lax.rem(me + step, C)
        pl.semaphore_signal(barrier, inc=1, device_id={"chan": to}, device_id_type=MESH)
        return 0

    lax.fori_loop(1, C, greet, 0)
    for other in (y_next, y_last):
        pl.semaphore_signal(barrier, inc=1, device_id={"blk": other}, device_id_type=MESH)

    omega_copy = pltpu.make_async_copy(omega_hbm, gen_ref, in_sem.at[0])
    ham_copy = pltpu.make_async_copy(ham_hbm, ham_ref, in_sem.at[1])
    omega_copy.start()
    ham_copy.start()

    def rows(index):
        return pl.ds(index * PER, PER)

    def start_out(t):
        first = z * (L - 1) + place + 1 - idle_n

        def one(step, _):
            owner = lax.rem(first + step, OWNERS)
            plane = owner // (L - 1)
            to = plane * L + lax.rem(plane + 1 + lax.rem(owner, L - 1), L)
            pltpu.make_async_remote_copy(
                src_ref=os_ref.at[t, rows(owner)], dst_ref=or_ref.at[t, rows(me)],
                send_sem=os_sem.at[t], recv_sem=or_sem.at[t],
                device_id={"chan": to}, device_id_type=MESH,
            ).start()
            return 0

        lax.fori_loop(0, OWNERS - 1 + idle_n, one, 0)

        @pl.when(owns)
        def _():
            pltpu.make_async_copy(
                os_ref.at[t, rows(mine)], or_ref.at[t, rows(me)], or_sem.at[t]
            ).start()

    def start_back(t):
        def one(step, _):
            to = lax.rem(me + step, C)
            pltpu.make_async_remote_copy(
                src_ref=bs_ref.at[t, rows(to)], dst_ref=br_ref.at[t, rows(mine)],
                send_sem=bs_sem.at[t], recv_sem=br_sem.at[t],
                device_id={"chan": to}, device_id_type=MESH,
            ).start()
            return 0

        lax.fori_loop(1, C, one, 0)
        pltpu.make_async_copy(
            bs_ref.at[t, rows(me)], br_ref.at[t, rows(mine)], br_sem.at[t]
        ).start()

    def wait_rows(ref, count, sem):
        part = ref.at[pl.ds(0, count)]
        pltpu.make_async_copy(part, part, sem).wait()

    def send(t, value):
        code = encode(value, OUT_TOP[t])
        for b in range(2):
            os_ref[t, ROWS * b : ROWS * (b + 1), :] = pack(
                code[:, 256 * b : 256 * b + 128], code[:, 256 * b + 128 : 256 * b + 256]
            )
        tail_ref[...] = code[0:72, 512:WIDE] + pltpu.roll(code[72:144, 512:WIDE], 64, 1)
        os_ref[t, TAIL:LAST, :] = pack(tail_ref[0:40, :], tail_ref[32:72, :])
        os_ref[t, LAST:WORDS, :] = jnp.zeros((WORDS - LAST, 128), I32)

    def arrived(t):
        wait_rows(or_ref.at[t], C * PER, or_sem.at[t])
        for j in range(PER):
            for k, code in enumerate(unpack(or_ref[t, pl.ds(j, C, stride=PER), :])):
                at = slice(256 * j + 128 * k, 256 * j + 128 * (k + 1))
                x_hi[:, at], x_lo[:, at] = halves(decode(code, OUT_TOP[t]))

    def times(high, low):
        return dot(high[...], x_hi[...]) + (dot(high[...], x_lo[...]) + dot(low[...], x_hi[...]))

    def send_mixed(t, value):
        code = encode(value, BACK_TOP[t])
        for j in range(PER):
            bs_ref[t, pl.ds(j, C, stride=PER), :] = pack(
                code[:, 256 * j : 256 * j + 128], code[:, 256 * j + 128 : 256 * j + 256]
            )
        start_back(t)

    def take_block(t):
        wait_rows(br_ref.at[t], WORDS, br_sem.at[t])
        top = BACK_TOP[t]
        for b in range(2):
            for k, code in enumerate(unpack(br_ref[t, ROWS * b : ROWS * (b + 1), :])):
                block_ref[:, 256 * b + 128 * k : 256 * b + 128 * (k + 1)] = decode(code, top)
        first, second = unpack(br_ref[t, TAIL:LAST, :])
        tail_ref[0:40, :] = first
        tail_ref[32:72, :] = second
        tail = decode(tail_ref[...], top)
        block_ref[0:72, 512:576] = tail[:, 0:64]
        block_ref[72:144, 512:576] = pltpu.roll(tail, 64, 1)[:, 0:64]
        return block_ref[...]

    def permuted(value, matrix):
        high, low = halves(value)
        return dot(high, matrix[...]) + dot(low, matrix[...])

    CUT = 80

    def y_copy(g, k, rows, to):
        return pltpu.make_async_remote_copy(
            src_ref=rows, dst_ref=rows,
            send_sem=ys_sem.at[g, k], recv_sem=yr_sem.at[g, k],
            device_id={"blk": to}, device_id_type=MESH,
        )

    def own_rows(g, who):
        return full.at[g, who]

    def upper(g, who):
        return full.at[g, who, pl.ds(0, CUT)]

    def lower(g, who):
        return full.at[g, who, pl.ds(CUT, ROWS - CUT)]

    def y_send(g):
        y_copy(g, 0, own_rows(g, y), y_next).start()
        y_copy(g, 1, own_rows(g, y), y_last).start()

    def y_start(g, value):
        full[g, y] = value
        y_send(g)

    def y_relay(g):
        y_copy(g, 0, own_rows(g, y_last), y_next).wait_recv()
        y_copy(g, 2, upper(g, y_last), y_next).start()
        y_copy(g, 1, own_rows(g, y_next), y_last).wait_recv()
        y_copy(g, 3, lower(g, y_next), y_last).start()

    def y_finish(g):
        far = lax.rem(y + 2, Y)
        y_copy(g, 2, upper(g, far), y_next).wait_recv()
        y_copy(g, 3, lower(g, far), y_last).wait_recv()

    def whole(g):
        return full[g].reshape(Y * ROWS, WIDTH)

    size = block[0]
    row_at = lax.broadcasted_iota(I32, (ROWS, WIDTH), 0) + y * ROWS
    col_at = lax.broadcasted_iota(I32, (ROWS, WIDTH), 1)
    inside = ((row_at < size) & (col_at < size)).astype(F32)
    cmap_row = cmap[...]
    perm[:, 0:WIDTH] = (
        lax.broadcasted_iota(I32, (WIDTH, WIDTH), 0) == cmap_row
    ).astype(F32).astype(BF16)
    perm[:, WIDTH:WIDE] = jnp.zeros((WIDTH, WIDE - WIDTH), BF16)

    omega_copy.wait()
    gen = gen_ref[...] * inside
    gen_ref[...] = gen
    send(G, permuted(gen, perm))
    ham_copy.wait()
    ham = ham_ref[...] * inside
    ham_ref[...] = ham
    send(H, permuted(ham, perm))
    full[YG, y] = gen.astype(BF16)
    full[YH, y] = ham.astype(BF16)
    pl.semaphore_wait(barrier, C - 1 + 2)
    start_out(G)
    y_send(YG)
    start_out(H)
    y_send(YH)

    exact = lax.Precision.HIGHEST

    def exact_dot(a, b, dims):
        return lax.dot_general(a, b, (dims, ((), ())), precision=exact, preferred_element_type=F32)

    jl = jnp.broadcast_to(jrow[...], (128, 128)).astype(F32)
    fam = jnp.broadcast_to(frow[...], (128, 128)).astype(F32)
    one_hot_t = (lax.broadcasted_iota(jnp.int32, (128, 128), 0).astype(F32) == jl).astype(F32)
    picked = exact_dot(sixj[...], one_hot_t, ((1,), (0,)))
    picked = exact_dot(one_hot_t.T, picked, ((1,), (0,)))
    mixing = picked * (fam == fam.T).astype(F32)
    mix_hi[...], mix_lo[...] = halves(mixing)
    reverse = mixing.T
    rev_hi[...], rev_lo[...] = halves(reverse)
    sq_hi[...], sq_lo[...] = halves(exact_dot(mixing, reverse, ((1,), (0,))))

    cmap_f = cmap_row.astype(F32)
    for b in range(5):
        span = min(128, WIDTH - 128 * b)
        piece = jnp.broadcast_to(cmap_f[:, 128 * b : 128 * b + span], (128, span)).T
        for k in range(5):
            span_k = min(128, WIDTH - 128 * k)
            at = (lax.broadcasted_iota(jnp.int32, (span, 128), 1) + 128 * k).astype(F32)
            unperm[128 * b : 128 * b + span, 128 * k : 128 * k + span_k] = (
                (piece == at).astype(F32).astype(BF16)[:, 0:span_k]
            )

    gen_s[...] = (gen_ref[...] * pair_w[...]).astype(BF16)
    ham_s[...] = (ham_ref[...] * pair_w[...]).astype(BF16)

    y_relay(YG)
    y_relay(YH)

    @pl.when(owns)
    def _():
        arrived(G)
        send_mixed(GB, times(mix_hi, mix_lo))
        arrived(H)
        send_mixed(HB, times(mix_hi, mix_lo))

    y_finish(YG)
    y_finish(YH)
    pp_ref[...] = dot(gen_s[...], whole(YH)) - dot(ham_s[...], whole(YG))
    send(PP, permuted(pp_ref[...], perm))
    start_out(PP)

    gc = take_block(GB)
    y_start(YGC, gc.astype(BF16))
    gc_s[...] = (gc * cross_w[...]).astype(BF16)
    hc = take_block(HB)
    y_start(YHC, hc.astype(BF16))
    hc_s[...] = (hc * cross_w[...]).astype(BF16)
    y_relay(YGC)
    y_relay(YHC)

    @pl.when(owns)
    def _():
        arrived(PP)
        comb_ref[...] = times(mix_hi, mix_lo)

    y_finish(YGC)
    y_finish(YHC)
    wide_ref[:, 512:WIDE] = jnp.zeros((ROWS, WIDE - 512), F32)
    wide_ref[:, 0:WIDTH] = dot(gc_s[...], whole(YHC)) - dot(hc_s[...], whole(YGC))
    send(CC, wide_ref[...])
    start_out(CC)

    @pl.when(owns)
    def _():
        arrived(CC)
        send_mixed(EB, comb_ref[...] + times(sq_hi, sq_lo))
        send_mixed(RB, times(rev_hi, rev_lo))

    ec = take_block(EB)
    y_start(YEC, ec.astype(BF16))
    hc_s[...] = (ec * cross_w[...]).astype(BF16)
    y_relay(YEC)
    y_finish(YEC)
    wide_ref[:, 0:WIDTH] = dot(gc_s[...], whole(YEC)) - dot(hc_s[...], whole(YGC))
    send(SO, wide_ref[...])
    start_out(SO)

    eta = pp_ref[...] + permuted(take_block(RB), unperm)
    eta_ref[...] = eta
    y_start(YE, eta.astype(BF16))
    ham_s[...] = (eta * pair_w[...]).astype(BF16)
    y_relay(YE)

    @pl.when(owns)
    def _():
        arrived(SO)
        send_mixed(SB, times(rev_hi, rev_lo))

    y_finish(YE)
    pp_ref[...] = dot(gen_s[...], whole(YE)) - dot(ham_s[...], whole(YG))
    second = pp_ref[...] + permuted(take_block(SB), unperm)
    out[...] = (ham_ref[...] + eta_ref[...] + 0.5 * second) * inside

    for t in range(5):
        wait_rows(os_ref.at[t], (OWNERS - 1) * PER, os_sem.at[t])

    @pl.when(idle)
    def _():
        for t in range(5):
            wait_rows(os_ref.at[t], PER, os_sem.at[t])

    @pl.when(owns)
    def _():
        for t in range(5):
            wait_rows(bs_ref.at[t], (C - 1) * PER, bs_sem.at[t])

    for g in range(6):
        y_copy(g, 0, own_rows(g, y), y_next).wait_send()
        y_copy(g, 1, own_rows(g, y), y_last).wait_send()
        y_copy(g, 2, upper(g, y_last), y_next).wait_send()
        y_copy(g, 3, lower(g, y_next), y_last).wait_send()


def on_device(omega, hamiltonian, pair_occ, cross_occ, block_size, jlabel, family, sixj, column_map):
    vmem = pl.BlockSpec(memory_space=pltpu.VMEM)
    hbm = pl.BlockSpec(memory_space=pltpu.MemorySpace.HBM)
    smem = pl.BlockSpec(memory_space=pltpu.SMEM)
    square = pltpu.VMEM((128, 128), BF16)
    rows_f = pltpu.VMEM((ROWS, WIDTH), F32)
    rows_b = pltpu.VMEM((ROWS, WIDTH), BF16)
    result = pl.pallas_call(
        kernel,
        out_shape=jax.ShapeDtypeStruct((ROWS, WIDTH), F32),
        in_specs=[hbm, hbm, vmem, vmem, smem, vmem, vmem, vmem, vmem],
        out_specs=vmem,
        scratch_shapes=[
            pltpu.VMEM((5, WORDS, 128), I32),
            pltpu.VMEM((5, C * PER, 128), I32),
            pltpu.VMEM((5, C * PER, 128), I32),
            pltpu.VMEM((5, WORDS, 128), I32),
            pltpu.VMEM((6, Y, ROWS, WIDTH), BF16),
            pltpu.VMEM((WIDTH, WIDE), BF16),
            pltpu.VMEM((WIDTH, WIDTH), BF16),
            square, square, square, square, square, square,
            pltpu.VMEM((ROWS, WIDE), F32),
            rows_f,
            pltpu.VMEM((72, 128), I32),
            pltpu.VMEM((C, 768), BF16),
            pltpu.VMEM((C, 768), BF16),
            rows_f, rows_f, rows_f,
            pltpu.VMEM((C, 768), F32),
            rows_b, rows_b, rows_b, rows_b,
            rows_f,
            pltpu.SemaphoreType.DMA((2,)),
            pltpu.SemaphoreType.DMA((5,)),
            pltpu.SemaphoreType.DMA((5,)),
            pltpu.SemaphoreType.DMA((5,)),
            pltpu.SemaphoreType.DMA((5,)),
            pltpu.SemaphoreType.DMA((6, 4)),
            pltpu.SemaphoreType.DMA((6, 4)),
        ],
        compiler_params=pltpu.CompilerParams(
            collective_id=0, has_side_effects=True, vmem_limit_bytes=48 * 1024 * 1024
        ),
    )(
        omega.reshape(ROWS, WIDTH),
        hamiltonian.reshape(ROWS, WIDTH),
        pair_occ,
        cross_occ,
        block_size,
        jlabel.reshape(1, 128),
        family.reshape(1, 128),
        sixj,
        column_map.reshape(1, WIDTH),
    )
    return result.reshape(1, ROWS, WIDTH)


def solution(mesh):
    in_specs = (
        P("chan", "blk", None),
        P("chan", "blk", None),
        P("chan", None),
        P("chan", None),
        P("chan"),
        P(),
        P(),
        P(),
        P(),
    )
    return jax.shard_map(
        on_device, mesh=mesh, in_specs=in_specs, out_specs=P("chan", "blk", None), check_vma=False
    )
```

time: 372 us -> 148 us (0.40)
  blocking collectives: 208 us -> 0 us
  Pallas kernels: 0 us -> 142 us
  waiting for transfers between devices: 55.5 us -> 0 us
  starting transfers between devices: 43.8 us -> 0 us
  local copies, waits for them, and re-layouts: 44.6 us -> 4.92 us
  matrix products: 8.38 us -> 0 us
  other arithmetic: 7.91 us -> 0 us
    all_to_all x3 -> x0, blocking collectives: 144 us -> none  [the longest x2 93.1 us: through_mixing(): lax.all_to_all(shaped, 'chan', split_axis=2, concat_axis=1, tiled=True)]
    pallas_call x0 -> x1, Pallas kernels: none -> 142 us  [on_device(): pl.pallas_call(kernel, out_shape=jax.ShapeDtypeStruct((ROWS, WIDTH), F32)...]
    all_gather x5 -> x0, blocking collectives: 63.9 us -> none  [the longest x4 51 us: commutator(): lax.all_gather(right_rows.astype(jnp.bfloat16), 'blk', axis=1, tiled=True)]
    all_to_all x4 -> x0, waiting for transfers between devices: 55.5 us -> none  [the longest x1 40.9 us: through_mixing(): lax.all_to_all(shaped, 'chan', split_axis=2, concat_axis=1, tiled=True)]
    all_to_all x4 -> x0, starting transfers between devices: 43.8 us -> none  [the longest x1 20.5 us: through_mixing(): lax.all_to_all(shaped, 'chan', split_axis=2, concat_axis=1, tiled=True)]
    gather x10 -> x0, local copies, waits for them, and re-layouts: 13.6 us -> none  [the longest x2 4.14 us: on_device(): second = second_pp + second_back[:, :, inverse_map]]
    another operation x10 -> x0, local copies, waits for them, and re-layouts: 9.25 us -> none  [the longest x3 3.37 us: on_device(): jnp.stack([first_pp[:, :, column_map], first_cc])]
    dot_general x14 -> x0, matrix products: 8.38 us -> none  [the longest x4 2.92 us: commutator(): jnp.einsum('crk,ckq->crq', scaled_right, left_full, preferred_element_typ...]
  transfers between devices with their start and end apart: 4 -> 0, of which waited for: 3 -> 0; matrix products, arithmetic and copies ran while one was open for 4% -> 0% of each run, Pallas kernels for 0% -> 0%
where the time goes in v1:
time: 148 us
  Pallas kernels  142 us (96%)
  local copies, waits for them, and re-layouts  4.92 us (3%)
    pallas_call x1, Pallas kernels, on_device(): pl.pallas_call(kernel, out_shape=jax.ShapeDtypeStruct((ROWS, WIDTH), F32)...  142 us
    unnamed x17, local copies, waits for them, and re-layouts  4.92 us

profile of v1, /device:TPU:1, one launch (start us, length us, event | category | flops | bytes accessed | tf_op | source)
XLA Modules:
  0.0 147.9 jit_solution(16899786309339818409)
XLA Ops:
  0.7 0.0 copy-start.7
  0.7 0.7 copy-done.7
  1.3 0.0 copy-start.3
  1.3 0.0 copy-start.4
  1.3 0.0 copy-start.5
  1.3 0.0 copy-start.6
  1.4 0.7 copy-done.3
  2.0 0.0 copy-done.4
  2.0 0.0 copy-done.5
  2.0 0.0 copy-done.6
  2.0 0.0 copy-start
  2.0 1.0 copy-done
  3.0 0.0 copy-start.1
  3.0 1.0 copy-done.1
  4.0 0.0 copy-start.2
  4.0 0.8 copy-done.2
  4.9 142.3 %shard_map.91 = f32[144,576]{1,0:T(8,128)S(1)} custom-call(f32[144,576]{1,0:T(8,128)S(1)} %bitcast.6, f32[144,576]{1,0:T(8,128)S(1)} %bitcast.7, f32[1,576]{1,0:T(1,128)S(1)} %copy-done.3, f32[1,576]{1,0:T(1,128)S(1)} %copy-done.4, s32[1]{0:T(128)S(6)} %copy.11.block, s32[1,128]{1,0:T(1,128)S(1)} %bitcast.8, s32[1,128]{1,0:T(1,128)S(1)} %bitcast.9, ...), custom_call_target="tpu_custom_call" | custom-call | tf_op jit(solution)/shard_map/pallas_call | solution.py:390
  147.2 0.7 copy.12
  (1 shorter events, 0.0 us)
Async XLA Ops:
  0.7 0.7 copy-start.7
  1.3 0.7 copy-start.3
  1.3 0.7 copy-start.4
  1.3 0.7 copy-start.5
  1.3 0.7 copy-start.6
  2.0 1.0 copy-start
  3.0 1.0 copy-start.1
  4.0 0.8 copy-start.2

commit v2 on v1

v2 whole, which is shorter than its diff:
```python
import math

import jax
import jax.numpy as jnp
from jax import lax
from jax.experimental import pallas as pl
from jax.experimental.pallas import tpu as pltpu
from jax.sharding import PartitionSpec as P

F32 = jnp.float32
BF16 = jnp.bfloat16
I32 = jnp.int32
MESH = pl.DeviceIdType.MESH

C = 128
L = 8
Y = 4
ROWS = 144
WIDTH = 576
WIDE = 640
PER = 3
OWNERS = 112
WORDS = OWNERS * PER
TAIL = 40
SPLIT = 184
LAST = 328
CUT_COL = 256

G, H, PP, CC, SO = range(5)
GB, HB, EB, RB, SB = range(5)
YG, YH, YGC, YHC, YE, YEC = range(6)

FLOOR = -126.0
OUT_TOP = (0.25, 6.0, 2.0**11, 2.0**26, 2.0**55)
BACK_TOP = (2.0**6, 2.0**11, 2.0**40, 2.0**34, 2.0**63)


def per_octave(top):
    return 32766.0 / (math.log2(top) - FLOOR)


def dot(a, b):
    return jnp.dot(a, b, preferred_element_type=F32)


def halves(value):
    high = value.astype(BF16)
    return high, (value - high.astype(F32)).astype(BF16)


def encode(value, top):
    scale = per_octave(top)
    size = jnp.maximum(jnp.abs(value), 2.0**FLOOR)
    code = jnp.minimum(jnp.round((jnp.log2(size) - FLOOR) * scale), 32767.0)
    return jnp.where(value < 0, -code, code).astype(I32)


def decode(code, top):
    value = code.astype(F32)
    size = jnp.exp2(jnp.abs(value) * (1.0 / per_octave(top)) + FLOOR)
    size = jnp.where(value < 0, -size, size)
    return jnp.where(value == 0, 0.0, size)


def pack(first, second):
    return lax.shift_left(first, 16) | (second & 0xFFFF)


def unpack(word):
    first = lax.shift_right_arithmetic(word, 16)
    return first, lax.shift_right_arithmetic(lax.shift_left(word, 16), 16)


def kernel(
    omega_hbm, ham_hbm, pair_hbm, cross_hbm, block, jrow_hbm, frow_hbm, sixj_hbm, cmap_hbm,
    out,
    os_ref, or_ref, bs_ref, br_ref,
    full_a, full_b, perm, unperm, mix_hi, mix_lo, rev_hi, rev_lo, sq_hi, sq_lo,
    wide_ref, block_ref, tail_ref, x_hi, x_lo,
    gen_ref, ham_ref, pp_ref, comb_ref, gen_s, ham_s, gc_s, hc_s, eta_ref,
    pair_w, cross_w, jrow, frow, sixj, cmap,
    in_sem, os_sem, or_sem, bs_sem, br_sem, ys_sem, yr_sem,
):
    me = lax.axis_index("chan")
    y = lax.axis_index("blk")
    z = me // L
    lane = lax.rem(me, L)
    place = lax.rem(lane - z - 1 + 3 * L, L)
    owns = place < L - 1
    idle = place == L - 1
    mine = z * (L - 1) + jnp.minimum(place, L - 2)
    idle_n = place // (L - 1)
    y_next = lax.rem(y + 1, Y)
    y_last = lax.rem(y + Y - 1, Y)

    barrier = pltpu.get_barrier_semaphore()

    def greet(step, _):
        to = lax.rem(me + step, C)
        pl.semaphore_signal(barrier, inc=1, device_id={"chan": to}, device_id_type=MESH)
        return 0

    lax.fori_loop(1, C, greet, 0)
    for other in (y_next, y_last):
        pl.semaphore_signal(barrier, inc=1, device_id={"blk": other}, device_id_type=MESH)

    pairs = (
        (cmap_hbm, cmap), (omega_hbm, gen_ref), (ham_hbm, ham_ref), (jrow_hbm, jrow),
        (frow_hbm, frow), (sixj_hbm, sixj), (pair_hbm, pair_w), (cross_hbm, cross_w),
    )
    loads = [pltpu.make_async_copy(a, b, in_sem.at[k]) for k, (a, b) in enumerate(pairs)]
    for load in loads:
        load.start()

    os_rows = os_ref.reshape(5, PER, OWNERS, 128)
    br_rows = br_ref.reshape(5, PER, OWNERS, 128)

    def pick(ref, t, j, n, index):
        return ref.at[t, pl.ds(j, n), pl.ds(index, 1)]

    def start_out(t, j, n):
        first = z * (L - 1) + place + 1 - idle_n

        def one(step, _):
            owner = lax.rem(first + step, OWNERS)
            plane = owner // (L - 1)
            to = plane * L + lax.rem(plane + 1 + lax.rem(owner, L - 1), L)
            pltpu.make_async_remote_copy(
                src_ref=pick(os_rows, t, j, n, owner), dst_ref=pick(or_ref, t, j, n, me),
                send_sem=os_sem.at[t, j], recv_sem=or_sem.at[t, j],
                device_id={"chan": to}, device_id_type=MESH,
            ).start()
            return 0

        lax.fori_loop(0, OWNERS - 1 + idle_n, one, 0)

        @pl.when(owns)
        def _():
            pltpu.make_async_copy(
                pick(os_rows, t, j, n, mine), pick(or_ref, t, j, n, me), or_sem.at[t, j]
            ).start()

    def start_back(t, j, n):
        def one(step, _):
            to = lax.rem(me + step, C)
            pltpu.make_async_remote_copy(
                src_ref=pick(bs_ref, t, j, n, to), dst_ref=pick(br_rows, t, j, n, mine),
                send_sem=bs_sem.at[t, j], recv_sem=br_sem.at[t, j],
                device_id={"chan": to}, device_id_type=MESH,
            ).start()
            return 0

        lax.fori_loop(1, C, one, 0)
        pltpu.make_async_copy(
            pick(bs_ref, t, j, n, me), pick(br_rows, t, j, n, mine), br_sem.at[t, j]
        ).start()

    def wait_rows(ref, t, j, n, count, sem):
        part = ref.at[t, pl.ds(j, n), pl.ds(0, count)]
        pltpu.make_async_copy(part, part, sem.at[t, j]).wait()

    def put_a(t, value):
        code = encode(value, OUT_TOP[t])
        tail_ref[...] = code[0:72, 256:384] + pltpu.roll(code[72:144, 256:384], 64, 1)
        os_ref[t, 0:TAIL, :] = pack(tail_ref[0:40, :], tail_ref[32:72, :])
        os_ref[t, TAIL:SPLIT, :] = pack(code[:, 0:128], code[:, 128:256])

    def put_b(t, value):
        code = encode(value, OUT_TOP[t])
        os_ref[t, SPLIT:LAST, :] = pack(code[:, 0:128], code[:, 128:256])
        os_ref[t, LAST:WORDS, :] = jnp.zeros((WORDS - LAST, 128), I32)

    def send(t, value):
        put_a(t, value[:, CUT_COL:WIDE])
        put_b(t, value[:, 0:CUT_COL])
        start_out(t, 0, PER)

    def arrived(t, j, n):
        wait_rows(or_ref, t, j, n, C, or_sem)
        for row in range(j, j + n):
            for k, code in enumerate(unpack(or_ref[t, row])):
                at = slice(256 * row + 128 * k, 256 * row + 128 * (k + 1))
                x_hi[:, at], x_lo[:, at] = halves(decode(code, OUT_TOP[t]))

    def times(high, low, j, n):
        at = slice(256 * j, 256 * (j + n))
        return dot(high[...], x_hi[:, at]) + (dot(high[...], x_lo[:, at]) + dot(low[...], x_hi[:, at]))

    def put_mixed(t, j, n, value):
        code = encode(value, BACK_TOP[t])
        for row in range(n):
            bs_ref[t, j + row] = pack(
                code[:, 256 * row : 256 * row + 128], code[:, 256 * row + 128 : 256 * row + 256]
            )

    def send_mixed(t, j, n, value):
        put_mixed(t, j, n, value)
        start_back(t, j, n)

    def back(t, j, n):
        wait_rows(br_rows, t, j, n, OWNERS, br_sem)

    def take_a(t):
        top = BACK_TOP[t]
        first, second = unpack(br_ref[t, 0:TAIL, :])
        tail_ref[0:40, :] = first
        tail_ref[32:72, :] = second
        tail = decode(tail_ref[...], top)
        block_ref[0:72, 512:576] = tail[:, 0:64]
        block_ref[72:144, 512:576] = pltpu.roll(tail, 64, 1)[:, 0:64]
        first, second = unpack(br_ref[t, TAIL:SPLIT, :])
        block_ref[:, 256:384] = decode(first, top)
        block_ref[:, 384:512] = decode(second, top)

    def take_b(t):
        top = BACK_TOP[t]
        first, second = unpack(br_ref[t, SPLIT:LAST, :])
        block_ref[:, 0:128] = decode(first, top)
        block_ref[:, 128:256] = decode(second, top)

    def permuted(value, matrix):
        high, low = halves(value)
        return dot(high, matrix[...]) + dot(low, matrix[...])

    CUT = 80
    parts = (full_a, full_b)

    def y_copy(g, c, k, rows, to):
        return pltpu.make_async_remote_copy(
            src_ref=rows, dst_ref=rows,
            send_sem=ys_sem.at[2 * g + c, k], recv_sem=yr_sem.at[2 * g + c, k],
            device_id={"blk": to}, device_id_type=MESH,
        )

    def own_rows(g, c, who):
        return parts[c].at[g, who]

    def upper(g, c, who):
        return parts[c].at[g, who, pl.ds(0, CUT)]

    def lower(g, c, who):
        return parts[c].at[g, who, pl.ds(CUT, ROWS - CUT)]

    def y_send(g, c):
        y_copy(g, c, 0, own_rows(g, c, y), y_next).start()
        y_copy(g, c, 1, own_rows(g, c, y), y_last).start()

    def y_start(g, c, value):
        parts[c][g, y] = value.astype(BF16)
        y_send(g, c)

    def y_relay(g, c):
        y_copy(g, c, 0, own_rows(g, c, y_last), y_next).wait_recv()
        y_copy(g, c, 2, upper(g, c, y_last), y_next).start()
        y_copy(g, c, 1, own_rows(g, c, y_next), y_last).wait_recv()
        y_copy(g, c, 3, lower(g, c, y_next), y_last).start()

    def y_finish(g, c):
        far = lax.rem(y + 2, Y)
        y_copy(g, c, 2, upper(g, c, far), y_next).wait_recv()
        y_copy(g, c, 3, lower(g, c, far), y_last).wait_recv()

    def whole(g, c):
        return parts[c][g].reshape(Y * ROWS, parts[c].shape[-1])

    size = block[0]
    row_at = lax.broadcasted_iota(I32, (ROWS, WIDTH), 0) + y * ROWS
    col_at = lax.broadcasted_iota(I32, (ROWS, WIDTH), 1)
    inside = ((row_at < size) & (col_at < size)).astype(F32)
    loads[0].wait()
    cmap_row = cmap[...].reshape(1, WIDTH)
    perm[:, 0:WIDTH] = (
        lax.broadcasted_iota(I32, (WIDTH, WIDTH), 0) == cmap_row
    ).astype(F32).astype(BF16)
    perm[:, WIDTH:WIDE] = jnp.zeros((WIDTH, WIDE - WIDTH), BF16)

    loads[1].wait()
    gen = gen_ref[...] * inside
    gen_ref[...] = gen
    value = permuted(gen, perm)
    put_a(G, value[:, CUT_COL:WIDE])
    put_b(G, value[:, 0:CUT_COL])
    full_a[YG, y] = gen[:, CUT_COL:].astype(BF16)
    full_b[YG, y] = gen[:, 0:CUT_COL].astype(BF16)
    pl.semaphore_wait(barrier, C - 1 + 2)
    start_out(G, 0, PER)
    loads[2].wait()
    ham = ham_ref[...] * inside
    ham_ref[...] = ham
    send(H, permuted(ham, perm))
    y_send(YG, 0)
    y_send(YG, 1)
    y_start(YH, 0, ham[:, CUT_COL:])
    y_start(YH, 1, ham[:, 0:CUT_COL])
    for load in loads[3:]:
        load.wait()

    exact = lax.Precision.HIGHEST

    def exact_dot(a, b, dims):
        return lax.dot_general(a, b, (dims, ((), ())), precision=exact, preferred_element_type=F32)

    jl = jnp.broadcast_to(jrow[...], (128, 128)).astype(F32)
    fam = jnp.broadcast_to(frow[...], (128, 128)).astype(F32)
    one_hot_t = (lax.broadcasted_iota(jnp.int32, (128, 128), 0).astype(F32) == jl).astype(F32)
    picked = exact_dot(sixj[...], one_hot_t, ((1,), (0,)))
    picked = exact_dot(one_hot_t.T, picked, ((1,), (0,)))
    mixing = picked * (fam == fam.T).astype(F32)
    mix_hi[...], mix_lo[...] = halves(mixing)
    reverse = mixing.T
    rev_hi[...], rev_lo[...] = halves(reverse)
    sq_hi[...], sq_lo[...] = halves(exact_dot(mixing, reverse, ((1,), (0,))))

    cmap_f = cmap_row.astype(F32)
    for b in range(5):
        span = min(128, WIDTH - 128 * b)
        piece = jnp.broadcast_to(cmap_f[:, 128 * b : 128 * b + span], (128, span)).T
        for k in range(5):
            span_k = min(128, WIDTH - 128 * k)
            at = (lax.broadcasted_iota(jnp.int32, (span, 128), 1) + 128 * k).astype(F32)
            unperm[128 * b : 128 * b + span, 128 * k : 128 * k + span_k] = (
                (piece == at).astype(F32).astype(BF16)[:, 0:span_k]
            )

    gen_s[...] = (gen_ref[...] * pair_w[...]).astype(BF16)
    ham_s[...] = (ham_ref[...] * pair_w[...]).astype(BF16)

    for g in (YG, YH):
        for c in range(2):
            y_relay(g, c)

    @pl.when(owns)
    def _():
        arrived(G, 0, PER)
        send_mixed(GB, 0, PER, times(mix_hi, mix_lo, 0, PER))
        arrived(H, 0, PER)
        put_mixed(HB, 0, PER, times(mix_hi, mix_lo, 0, PER))
        start_back(HB, 0, 2)
        start_back(HB, 2, 1)

    for g in (YG, YH):
        for c in range(2):
            y_finish(g, c)

    def commuted(first, second_full, second, first_full, c):
        return dot(first[...], whole(second_full, c)) - dot(second[...], whole(first_full, c))

    pp_ref[:, CUT_COL:] = commuted(gen_s, YH, ham_s, YG, 0)
    pp_ref[:, 0:CUT_COL] = commuted(gen_s, YH, ham_s, YG, 1)
    send(PP, permuted(pp_ref[...], perm))

    def take_and_gather(t, g):
        take_a(t)
        y_start(g, 0, block_ref[:, CUT_COL:])

    def take_rest(t, g):
        take_b(t)
        y_start(g, 1, block_ref[:, 0:CUT_COL])

    back(GB, 0, PER)
    take_and_gather(GB, YGC)
    take_rest(GB, YGC)
    gc_s[...] = (block_ref[...] * cross_w[...]).astype(BF16)
    y_relay(YGC, 0)
    y_relay(YGC, 1)
    back(HB, 0, 2)
    take_and_gather(HB, YHC)
    back(HB, 2, 1)
    take_rest(HB, YHC)
    hc_s[...] = (block_ref[...] * cross_w[...]).astype(BF16)
    y_relay(YHC, 0)
    y_relay(YHC, 1)

    @pl.when(owns)
    def _():
        arrived(PP, 0, PER)
        comb_ref[...] = times(mix_hi, mix_lo, 0, PER)

    wide_ref[:, 256:384] = jnp.zeros((ROWS, 128), F32)

    def cross_commutator(t, g):
        y_finish(g, 0)
        wide_ref[:, 0:320] = commuted(gc_s, g, hc_s, YGC, 0)
        put_a(t, wide_ref[...])
        start_out(t, 0, 1)
        y_finish(g, 1)
        put_b(t, commuted(gc_s, g, hc_s, YGC, 1))
        start_out(t, 1, 2)

    y_finish(YGC, 0)
    y_finish(YGC, 1)
    cross_commutator(CC, YHC)

    @pl.when(owns)
    def _():
        arrived(CC, 0, 1)
        send_mixed(EB, 0, 1, comb_ref[:, 0:256] + times(sq_hi, sq_lo, 0, 1))
        arrived(CC, 1, 2)
        put_mixed(EB, 1, 2, comb_ref[:, 256:768] + times(sq_hi, sq_lo, 1, 2))
        start_back(EB, 1, 1)
        start_back(EB, 2, 1)
        send_mixed(RB, 0, PER, times(rev_hi, rev_lo, 0, PER))

    back(EB, 0, 1)
    back(EB, 1, 1)
    take_and_gather(EB, YEC)
    back(EB, 2, 1)
    take_rest(EB, YEC)
    hc_s[...] = (block_ref[...] * cross_w[...]).astype(BF16)
    y_relay(YEC, 0)
    y_relay(YEC, 1)
    cross_commutator(SO, YEC)

    back(RB, 0, PER)
    take_a(RB)
    take_b(RB)
    eta = pp_ref[...] + permuted(block_ref[...], unperm)
    eta_ref[...] = eta
    y_start(YE, 0, eta[:, CUT_COL:])
    y_start(YE, 1, eta[:, 0:CUT_COL])
    ham_s[...] = (eta * pair_w[...]).astype(BF16)

    @pl.when(owns)
    def _():
        arrived(SO, 0, 1)
        send_mixed(SB, 0, 1, times(rev_hi, rev_lo, 0, 1))

    y_relay(YE, 0)
    y_relay(YE, 1)

    @pl.when(owns)
    def _():
        arrived(SO, 1, 2)
        send_mixed(SB, 1, 2, times(rev_hi, rev_lo, 1, 2))

    y_finish(YE, 0)
    y_finish(YE, 1)
    pp_ref[:, CUT_COL:] = commuted(gen_s, YE, ham_s, YG, 0)
    pp_ref[:, 0:CUT_COL] = commuted(gen_s, YE, ham_s, YG, 1)
    back(SB, 0, 1)
    back(SB, 1, 2)
    take_a(SB)
    take_b(SB)
    second = pp_ref[...] + permuted(block_ref[...], unperm)
    out[...] = (ham_ref[...] + eta_ref[...] + 0.5 * second) * inside

    out_cuts = ((G, 0, PER), (H, 0, PER), (PP, 0, PER), (CC, 0, 1), (CC, 1, 2), (SO, 0, 1), (SO, 1, 2))
    back_cuts = (
        (GB, 0, PER), (HB, 0, 2), (HB, 2, 1), (EB, 0, 1), (EB, 1, 1), (EB, 2, 1),
        (RB, 0, PER), (SB, 0, 1), (SB, 1, 2),
    )
    for cut in out_cuts:
        wait_rows(os_rows, *cut, OWNERS - 1, os_sem)

    @pl.when(idle)
    def _():
        for cut in out_cuts:
            wait_rows(os_rows, *cut, 1, os_sem)

    @pl.when(owns)
    def _():
        for cut in back_cuts:
            wait_rows(bs_ref, *cut, C - 1, bs_sem)

    for g in range(6):
        for c in range(2):
            y_copy(g, c, 0, own_rows(g, c, y), y_next).wait_send()
            y_copy(g, c, 1, own_rows(g, c, y), y_last).wait_send()
            y_copy(g, c, 2, upper(g, c, y_last), y_next).wait_send()
            y_copy(g, c, 3, lower(g, c, y_next), y_last).wait_send()


def on_device(omega, hamiltonian, pair_occ, cross_occ, block_size, jlabel, family, sixj, column_map):
    vmem = pl.BlockSpec(memory_space=pltpu.VMEM)
    hbm = pl.BlockSpec(memory_space=pltpu.MemorySpace.HBM)
    smem = pl.BlockSpec(memory_space=pltpu.SMEM)
    square = pltpu.VMEM((128, 128), BF16)
    rows_f = pltpu.VMEM((ROWS, WIDTH), F32)
    rows_b = pltpu.VMEM((ROWS, WIDTH), BF16)
    result = pl.pallas_call(
        kernel,
        out_shape=jax.ShapeDtypeStruct((ROWS, WIDTH), F32),
        in_specs=[hbm, hbm, hbm, hbm, smem, hbm, hbm, hbm, hbm],
        out_specs=vmem,
        scratch_shapes=[
            pltpu.VMEM((5, WORDS, 128), I32),
            pltpu.VMEM((5, PER, C, 128), I32),
            pltpu.VMEM((5, PER, C, 128), I32),
            pltpu.VMEM((5, WORDS, 128), I32),
            pltpu.VMEM((6, Y, ROWS, WIDTH - CUT_COL), BF16),
            pltpu.VMEM((6, Y, ROWS, CUT_COL), BF16),
            pltpu.VMEM((WIDTH, WIDE), BF16),
            pltpu.VMEM((WIDTH, WIDTH), BF16),
            square, square, square, square, square, square,
            pltpu.VMEM((ROWS, WIDE - CUT_COL), F32),
            rows_f,
            pltpu.VMEM((72, 128), I32),
            pltpu.VMEM((C, 768), BF16),
            pltpu.VMEM((C, 768), BF16),
            rows_f, rows_f, rows_f,
            pltpu.VMEM((C, 768), F32),
            rows_b, rows_b, rows_b, rows_b,
            rows_f,
            pltpu.VMEM((1, WIDTH), F32),
            pltpu.VMEM((1, WIDTH), F32),
            pltpu.VMEM((1, 128), I32),
            pltpu.VMEM((1, 128), I32),
            pltpu.VMEM((128, 128), F32),
            pltpu.VMEM((WIDTH,), I32),
            pltpu.SemaphoreType.DMA((8,)),
            pltpu.SemaphoreType.DMA((5, PER)),
            pltpu.SemaphoreType.DMA((5, PER)),
            pltpu.SemaphoreType.DMA((5, PER)),
            pltpu.SemaphoreType.DMA((5, PER)),
            pltpu.SemaphoreType.DMA((12, 4)),
            pltpu.SemaphoreType.DMA((12, 4)),
        ],
        compiler_params=pltpu.CompilerParams(
            collective_id=0, has_side_effects=True, vmem_limit_bytes=60 * 1024 * 1024
        ),
    )(
        omega.reshape(ROWS, WIDTH),
        hamiltonian.reshape(ROWS, WIDTH),
        pair_occ,
        cross_occ,
        block_size,
        jlabel.reshape(1, 128),
        family.reshape(1, 128),
        sixj,
        column_map,
    )
    return result.reshape(1, ROWS, WIDTH)


def solution(mesh):
    in_specs = (
        P("chan", "blk", None),
        P("chan", "blk", None),
        P("chan", None),
        P("chan", None),
        P("chan"),
        P(),
        P(),
        P(),
        P(),
    )
    return jax.shard_map(
        on_device, mesh=mesh, in_specs=in_specs, out_specs=P("chan", "blk", None), check_vma=False
    )
```

time: 148 us -> 139 us (0.939)
  Pallas kernels: 142 us -> 136 us
  local copies, waits for them, and re-layouts: 4.92 us -> 1.75 us
    pallas_call x1, Pallas kernels: 142 us -> 136 us  [on_device(): pl.pallas_call(kernel, out_shape=jax.ShapeDtypeStruct((ROWS, WIDTH), F32)...]
    unnamed x17 -> x1, local copies, waits for them, and re-layouts: 4.92 us -> 1.75 us
where the time goes in v2:
time: 139 us
  Pallas kernels  136 us (98%)
  local copies, waits for them, and re-layouts  1.75 us (1%)
    pallas_call x1, Pallas kernels, on_device(): pl.pallas_call(kernel, out_shape=jax.ShapeDtypeStruct((ROWS, WIDTH), F32)...  136 us

profile of v2, /device:TPU:1, one launch (start us, length us, event | category | flops | bytes accessed | tf_op | source)
XLA Modules:
  0.0 138.8 jit_solution(14795218066540790952)
XLA Ops:
  0.7 136.4 %shard_map.91 = f32[144,576]{1,0:T(8,128)} custom-call(f32[144,576]{1,0:T(8,128)} %bitcast.6, f32[144,576]{1,0:T(8,128)} %bitcast.7, f32[1,576]{1,0:T(1,128)} %pair_hbm.1, f32[1,576]{1,0:T(1,128)} %cross_hbm.1, s32[1]{0:T(128)S(6)} %copy.11.block, s32[1,128]{1,0:T(1,128)} %bitcast.8, s32[1,128]{1,0:T(1,128)} %bitcast.9, f32[128,128]{1,0:T(8,128)} %sixj_hbm.1, ...), custom_call_target="tpu_custom_call" | custom-call | tf_op jit(solution)/shard_map/pallas_call | solution.py:480
  137.1 1.7 %copy.12 = f32[1,144,576]{2,1,0:T(8,128)} copy(f32[1,144,576]{2,1,0:T(8,128)} %bitcast.5) | data formatting | bytes 663552

commit v3 on v2

--- a/solution.py
+++ b/solution.py
@@ -95,12 +95,16 @@
 
     barrier = pltpu.get_barrier_semaphore()
 
+    def far_first(step, middle):
+        half = (step + 1) // 2
+        return middle + jnp.where(lax.rem(step, 2) == 1, half, -half)
+
     def greet(step, _):
-        to = lax.rem(me + step, C)
+        to = lax.rem(me + far_first(step, C // 2), C)
         pl.semaphore_signal(barrier, inc=1, device_id={"chan": to}, device_id_type=MESH)
         return 0
 
-    lax.fori_loop(1, C, greet, 0)
+    lax.fori_loop(0, C - 1, greet, 0)
     for other in (y_next, y_last):
         pl.semaphore_signal(barrier, inc=1, device_id={"blk": other}, device_id_type=MESH)
 
@@ -119,10 +123,10 @@
         return ref.at[t, pl.ds(j, n), pl.ds(index, 1)]
 
     def start_out(t, j, n):
-        first = z * (L - 1) + place + 1 - idle_n
+        first = z * (L - 1) + place
 
         def one(step, _):
-            owner = lax.rem(first + step, OWNERS)
+            owner = lax.rem(first + far_first(step, OWNERS // 2), OWNERS)
             plane = owner // (L - 1)
             to = plane * L + lax.rem(plane + 1 + lax.rem(owner, L - 1), L)
             pltpu.make_async_remote_copy(
@@ -142,7 +146,7 @@
 
     def start_back(t, j, n):
         def one(step, _):
-            to = lax.rem(me + step, C)
+            to = lax.rem(me + far_first(step, C // 2), C)
             pltpu.make_async_remote_copy(
                 src_ref=pick(bs_ref, t, j, n, to), dst_ref=pick(br_rows, t, j, n, mine),
                 send_sem=bs_sem.at[t, j], recv_sem=br_sem.at[t, j],
@@ -150,7 +154,7 @@
             ).start()
             return 0
 
-        lax.fori_loop(1, C, one, 0)
+        lax.fori_loop(0, C - 1, one, 0)
         pltpu.make_async_copy(
             pick(bs_ref, t, j, n, me), pick(br_rows, t, j, n, mine), br_sem.at[t, j]
         ).start()
@@ -379,12 +383,14 @@
     wide_ref[:, 256:384] = jnp.zeros((ROWS, 128), F32)
 
     def cross_commutator(t, g):
+        wide_ref[:, 0:320] = dot(hc_s[...], whole(YGC, 0))
+        block_ref[:, 0:CUT_COL] = dot(hc_s[...], whole(YGC, 1))
         y_finish(g, 0)
-        wide_ref[:, 0:320] = commuted(gc_s, g, hc_s, YGC, 0)
+        wide_ref[:, 0:320] = dot(gc_s[...], whole(g, 0)) - wide_ref[:, 0:320]
         put_a(t, wide_ref[...])
         start_out(t, 0, 1)
         y_finish(g, 1)
-        put_b(t, commuted(gc_s, g, hc_s, YGC, 1))
+        put_b(t, dot(gc_s[...], whole(g, 1)) - block_ref[:, 0:CUT_COL])
         start_out(t, 1, 2)
 
     y_finish(YGC, 0)

time: 139 us -> 133 us (0.957)
  Pallas kernels: 136 us -> 131 us
    pallas_call x1, Pallas kernels: 136 us -> 131 us  [on_device(): pl.pallas_call(kernel, out_shape=jax.ShapeDtypeStruct((ROWS, WIDTH), F32)...]
where the time goes in v3:
time: 133 us
  Pallas kernels  131 us (98%)
  local copies, waits for them, and re-layouts  1.75 us (1%)
    pallas_call x1, Pallas kernels, on_device(): pl.pallas_call(kernel, out_shape=jax.ShapeDtypeStruct((ROWS, WIDTH), F32)...  131 us

profile of v3, /device:TPU:1, one launch (start us, length us, event | category | flops | bytes accessed | tf_op | source)
XLA Modules:
  0.0 133.2 jit_solution(10663078406366995765)
XLA Ops:
  0.7 130.8 %shard_map.91 = f32[144,576]{1,0:T(8,128)} custom-call(f32[144,576]{1,0:T(8,128)} %bitcast.6, f32[144,576]{1,0:T(8,128)} %bitcast.7, f32[1,576]{1,0:T(1,128)} %pair_hbm.1, f32[1,576]{1,0:T(1,128)} %cross_hbm.1, s32[1]{0:T(128)S(6)} %copy.11.block, s32[1,128]{1,0:T(1,128)} %bitcast.8, s32[1,128]{1,0:T(1,128)} %bitcast.9, f32[128,128]{1,0:T(8,128)} %sixj_hbm.1, ...), custom_call_target="tpu_custom_call" | custom-call | tf_op jit(solution)/shard_map/pallas_call | solution.py:486
  131.5 1.7 %copy.12 = f32[1,144,576]{2,1,0:T(8,128)} copy(f32[1,144,576]{2,1,0:T(8,128)} %bitcast.5) | data formatting | bytes 663552
